TPU v7x, 512 devices: a whole 4x4x16 slice. The times are simulated.
512 devices in a mesh: snap: 16 (over x, y), vert: 32 (over z, core).
Axes of the slice: x: 4, y: 4, z: 16, core: 2. Of those that a mesh axis runs over, the one named last changes fastest.
Arguments:
- features: bfloat16 [16, 16384, 256], P('snap', 'vert'), may hold values from -6 to 6
- tile_src: int32 [16, 1024], P('snap', 'vert'), may hold values from 0 to 127, as said below
- tile_dst: int32 [16, 1024], P('snap', 'vert'), may hold values from 0 to 127, as said below
- tile_count: int32 [16, 32], P('snap', 'vert'), may hold values from 4 to 32, as said below
- tile_vals: bfloat16 [16, 1024, 128, 128], P('snap', 'vert'), may hold values from -0.25 to 0.25
- norm_gain: float32 [256], replicated, may hold values from 0.25 to 1.75
- mix_weight: bfloat16 [256, 512], replicated, may hold values from -0.375 to 0.375
- decay_rate: float32 [16, 256], replicated, may hold values from 0 to 9, as said below
- mlp_gain: float32 [256], replicated, may hold values from 0.25 to 1.75
- up_weight: bfloat16 [256, 1024], replicated, may hold values from -0.375 to 0.375
- down_weight: bfloat16 [1024, 256], replicated, may hold values from -0.1875 to 0.1875
- link_weight: bfloat16 [256, 256], replicated, may hold values from -0.375 to 0.375
- pair_left: int32 [16, 1024], P('snap', 'vert'), may hold values from 0 to 127, as said below
- pair_right: int32 [16, 1024], P('snap', 'vert'), may hold values from 0 to 127, as said below
Outputs:
- embeddings: bfloat16 [16, 16384, 256], P('snap', 'vert')
- scores: bfloat16 [16, 1024, 128, 128], P('snap', 'vert')
Inputs may be any that keep to these rules, and one draw needn't show every extreme that they name: `tile_src`: a slot of vertex part p names a source block from p * 4 - 4 to p * 4 + 2 * 4 - 1. `tile_dst`: a slot of vertex part p names a destination block of that part, p * 4 to p * 4 + 3. `tile_count`: in every snapshot some vertex part has all 32 slots live. `decay_rate`: decay rates are positive. `pair_left`: a pair of vertex part p has its first block in that part, p * 4 to p * 4 + 3. `pair_right`: a pair of vertex part p has its second block from p * 4 - 4 to p * 4 + 2 * 4 - 1.
All inputs are finite; a program needn't handle non-finite values.
Results may differ from a plain program's by a relative error of at most 0.0091.
Values may be sent and summed in bfloat16 or wider, within the bound.
No kernel may reach another device: no remote copies, remote signals or barrier semaphores. Data moves between devices by JAX's collectives and lax.ppermute only.
A program may use at most 64 MiB of HBM per device.

v0:
```python
import jax
import jax.numpy as jnp
from jax import lax
from jax.sharding import PartitionSpec as P

epsilon = 1e-06


def with_halo(cells, sides, width):
    for axis, dim in sides:
        count = lax.axis_size(axis)
        ends = count - 1
        head = lax.slice_in_dim(cells, 0, width, axis=dim)
        tail = lax.slice_in_dim(cells, cells.shape[dim] - width, cells.shape[dim], axis=dim)
        cells = jnp.concatenate(
            [
                lax.ppermute(tail, axis, [(i, (i + 1) % count) for i in range(ends)]),
                cells,
                lax.ppermute(head, axis, [((i + 1) % count, i) for i in range(ends)]),
            ],
            axis=dim,
        )
    return cells


def root_norm(values, gain_vector):
    return (
        values
        * lax.rsqrt(jnp.mean(values * values, axis=-1, keepdims=True) + epsilon)
        * gain_vector
    )


def pick_blocks(blocks, indices):
    return jax.vmap(lambda source_table, chosen: jnp.take(source_table, chosen, axis=0))(
        blocks, indices
    )


def tile_terms(blocks, src_index, dst_index, tile_part, alive_slots, per_part):
    picked = pick_blocks(blocks, src_index)
    product = jnp.einsum("sgij,sgjf->sgif", tile_part, picked, preferred_element_type=jnp.float32)
    targets = jnp.arange(per_part, dtype=jnp.int32)[None, None, :]
    selector = ((dst_index[:, :, None] == targets) & alive_slots[:, :, None]).astype(jnp.float32)
    return jnp.einsum("sgb,sgif->sbif", selector, product, precision=lax.Precision.HIGHEST)


def gate_drive(normed, step_rates, mix_weight):
    projected = jnp.einsum("tnf,fg->tng", normed, mix_weight, preferred_element_type=jnp.float32)
    feature_width = normed.shape[-1]
    decays = jnp.exp(-step_rates[:, None, :] * jax.nn.sigmoid(projected[..., :feature_width]))
    return (decays, (1.0 - decays) * projected[..., feature_width:])


def advance(previous, inputs):
    updated = inputs[0] * previous + inputs[1]
    return (updated, updated)


def run_states(decays, drives, start_state):
    final_state, states = lax.scan(advance, start_state, (decays, drives))
    return states


def feed_forward(states, mlp_gain, up_weight, down_weight):
    state_normed = root_norm(states, mlp_gain).astype(jnp.bfloat16)
    hidden = jax.nn.silu(
        jnp.einsum("tnf,fh->tnh", state_normed, up_weight, preferred_element_type=jnp.float32)
    ).astype(jnp.bfloat16)
    return (
        states + jnp.einsum("tnh,hf->tnf", hidden, down_weight, preferred_element_type=jnp.float32)
    ).astype(jnp.bfloat16)


def body(
    features,
    tile_src,
    tile_dst,
    tile_count,
    tile_vals,
    norm_gain,
    mix_weight,
    decay_rate,
    mlp_gain,
    up_weight,
    down_weight,
    link_weight,
    pair_left,
    pair_right,
):
    snaps_here, vertices_here, feature_width = features.shape
    tile_rows = tile_vals.shape[-1]
    slot_count = tile_vals.shape[1]
    per_part = vertices_here // tile_rows
    part_index = lax.axis_index("vert")
    first_block = (part_index - 1) * per_part
    own_first = part_index * per_part
    extended = with_halo(features, (("vert", 1),), vertices_here)
    blocks = extended.reshape(snaps_here, 3 * per_part, tile_rows, feature_width)
    local_src = tile_src - first_block
    local_dst = tile_dst - own_first
    slot_ids = jnp.arange(slot_count, dtype=jnp.int32)[None, :]
    aggregate = tile_terms(blocks, local_src, local_dst, tile_vals, slot_ids < tile_count, per_part)
    combined = aggregate.reshape(snaps_here, vertices_here, feature_width) + features.astype(
        jnp.float32
    )
    normed = root_norm(combined, norm_gain).astype(jnp.bfloat16)
    by_vertex = lax.all_to_all(normed, "snap", split_axis=1, concat_axis=0, tiled=True)
    decays, drives = gate_drive(by_vertex, decay_rate, mix_weight)
    states = run_states(decays, drives, jnp.zeros(decays.shape[1:], jnp.float32))
    vertex_out = feed_forward(states, mlp_gain, up_weight, down_weight)
    embeddings = lax.all_to_all(vertex_out, "snap", split_axis=0, concat_axis=1, tiled=True)
    extended_out = with_halo(embeddings, (("vert", 1),), vertices_here)
    left_side = jnp.einsum(
        "svf,fg->svg", embeddings, link_weight, preferred_element_type=jnp.float32
    ).astype(jnp.bfloat16)
    left_blocks = pick_blocks(
        left_side.reshape(snaps_here, per_part, tile_rows, feature_width), pair_left - own_first
    )
    right_blocks = pick_blocks(
        extended_out.reshape(snaps_here, 3 * per_part, tile_rows, feature_width),
        pair_right - first_block,
    )
    scores = jnp.einsum(
        "spif,spjf->spij", left_blocks, right_blocks, preferred_element_type=jnp.float32
    ) * feature_width ** (-0.5)
    return (embeddings, scores.astype(jnp.bfloat16))


def solution(mesh):
    return jax.shard_map(
        body,
        mesh=mesh,
        in_specs=(
            P("snap", "vert", None),
            P("snap", "vert"),
            P("snap", "vert"),
            P("snap", "vert"),
            P("snap", "vert", None, None),
            P(),
            P(),
            P(),
            P(),
            P(),
            P(),
            P(),
            P("snap", "vert"),
            P("snap", "vert"),
        ),
        out_specs=(P("snap", "vert", None), P("snap", "vert", None, None)),
        check_vma=False,
    )
```

profile of v0, /device:TPU:97, one launch (start us, length us, event | category | flops | bytes accessed | tf_op | source)
XLA Modules:
  0.0 86.9 jit_solution(15219343378757450271)
XLA Ops:
  0.6 5.5 %collective-permute-start = (bf16[1,512,256]{2,1,0:T(8,128)(2,1)}, bf16[1,512,256]{2,1,0:T(8,128)(2,1)S(1)}, u32[]{:S(2)}, u32[]{:S(2)}) collective-permute-start(bf16[1,512,256]{2,1,0:T(8,128)(2,1)} %param.18), channel_id=1, source_target_pairs={{0,1},{1,2},{2,3},{3,4},{4,5},{5,6},{6,7},{7,8},{8,9},{9,10},{10,1... | collective-permute-start | bytes 786440 | tf_op jit(solution)/shard_map/ppermute | solution.py:17
  6.1 1.9 %collective-permute-start.1 = (bf16[1,512,256]{2,1,0:T(8,128)(2,1)}, bf16[1,512,256]{2,1,0:T(8,128)(2,1)S(1)}, u32[]{:S(2)}, u32[]{:S(2)}) collective-permute-start(bf16[1,512,256]{2,1,0:T(8,128)(2,1)} %param.18), channel_id=1, source_target_pairs={{1,0},{2,1},{3,2},{4,3},{5,4},{6,5},{7,6},{8,7},{9,8},{10,9},{11,1... | collective-permute-start | bytes 786440 | tf_op jit(solution)/shard_map/ppermute | solution.py:19
  8.0 0.7 and_bitcast_fusion.1
  9.4 0.7 subtract_bitcast_fusion
  10.0 0.7 neg.11
  10.8 4.4 %collective-permute-done.1 = bf16[1,512,256]{2,1,0:T(8,128)(2,1)S(1)} collective-permute-done((bf16[1,512,256]{2,1,0:T(8,128)(2,1)}, bf16[1,512,256]{2,1,0:T(8,128)(2,1)S(1)}, u32[]{:S(2)}, u32[]{:S(2)}) %collective-permute-start.1) | collective-permute-done | bytes 262176 | tf_op jit(solution)/shard_map/ppermute | solution.py:19
  15.2 1.0 %pad_maximum_fusion = bf16[1,1536,256]{2,1,0:T(8,128)(2,1)S(1)} fusion(bf16[1,512,256]{2,1,0:T(8,128)(2,1)S(1)} %collective-permute-done.1, bf16[1,512,256]{2,1,0:T(8,128)(2,1)} %param.18, bf16[1,512,256]{2,1,0:T(8,128)(2,1)S(1)} %collective-permute-done), kind=kLoop, calls=%fused_computation.27 | loop fusion | flops 2359296 | bytes 1572864 | tf_op jit(solution)/shard_map/concatenate | solution.py:15
  16.2 2.0 %gather_fusion.1 = bf16[32,128,256]{2,1,0:T(8,128)(2,1)} fusion(bf16[1,12,128,256]{3,2,1,0:T(8,128)(2,1)S(1)} %bitcast.104, s32[32]{0:T(128)S(1)} %or_bitcast_fusion.1), kind=kCustom, calls=%fused_computation.clone | custom fusion | bytes 4194560 | tf_op jit(solution)/shard_map/vmap(jit(_take))/gather | solution.py:35
  18.2 4.4 %convolution_bitcast_fusion = f32[32,128,256]{1,2,0:T(8,128)} fusion(bf16[32,128,256]{2,1,0:T(8,128)(2,1)} %gather_fusion.1, pred[32]{0:T(512)(128)(4,1)S(1)} %get-tuple-element.67, bf16[1,32,128,128]{3,2,1,0:T(8,128)(2,1)S(1)} %copy-done), kind=kOutput, calls=%fused_computation.6 | convolution fusion | flops 269484032 | bytes 7340064 | tf_op jit(solution)/shard_map/sgij,sgjf->sgif/dot_general | solution.py:42
  22.6 5.5 %copy.21 = f32[32,128,256]{2,0,1:T(8,128)} copy(f32[32,128,256]{1,2,0:T(8,128)} %convolution_bitcast_fusion) | data formatting | bytes 8388608 | tf_op jit(solution)/shard_map/sgij,sgjf->sgif/dot_general | solution.py:42
  28.1 3.7 %fusion.38 = f32[4,128,256]{2,0,1:T(4,128)S(1)} fusion(f32[32,128,256]{2,0,1:T(8,128)} %copy.21, s32[32]{0:T(128)S(1)} %subtract_bitcast_fusion, pred[32]{0:T(512)(128)(4,1)S(1)} %iota_compare_fusion.1), kind=kOutput, calls=%fused_computation.55 | convolution fusion | flops 50331904 | bytes 4718752 | tf_op jit(solution)/shard_map/sgb,sgif->sbif/dot_general | solution.py:45
  32.3 0.4 copy.27
  32.7 0.5 broadcast.170
  33.2 2.2 %reduce.1 = bf16[512,256]{1,0:T(8,128)(2,1)S(1)} reduce(bf16[512,1,256]{2,1,0:T(2,128)(2,1)S(1)} %bitcast.114, bf16[]{:T(256)} %broadcast.170), dimensions={1}, to_apply=%bitcast.97.reduce_sub_computation | reduce | bytes 524290
  35.4 0.8 reshape.205
  36.2 6.8 %all-to-all-start = ((bf16[16,2,4096]{2,1,0:T(2,128)(2,1)}), bf16[16,2,4096]{2,1,0:T(2,128)(2,1)S(1)}, u32[]{:S(2)}, u32[]{:S(2)}) async-start(bf16[16,2,4096]{2,1,0:T(2,128)(2,1)} %reshape.205), calls=%async_computation | async-start | bytes 524288 | tf_op jit(solution)/shard_map/all_to_all | solution.py:108
  43.0 7.3 %all-to-all-done = bf16[16,2,4096]{2,1,0:T(2,128)(2,1)S(1)} async-done(((bf16[16,2,4096]{2,1,0:T(2,128)(2,1)}), bf16[16,2,4096]{2,1,0:T(2,128)(2,1)S(1)}, u32[]{:S(2)}, u32[]{:S(2)}) %all-to-all-start) | async-done | bytes 262176 | tf_op jit(solution)/shard_map/all_to_all | solution.py:108
  50.3 0.3 reshape.206
  50.6 0.3 fusion.30
  50.9 0.2 slice_multiply_fusion
  51.1 0.6 while.13
  52.0 2.8 %fusion.16 = bf16[16,32,256]{2,1,0:T(8,128)(2,1)} fusion(f32[16,32,256]{2,1,0:T(8,128)S(1)} %get-tuple-element.30, bf16[1024,256]{1,0:T(8,128)(2,1)} %param.28, bf16[256,1024]{1,0:T(8,128)(2,1)} %param.27, f32[256]{0:T(256)S(1)} %copy-done.7, f32[16,32]{1,0:T(8,128)S(1)} %add_rsqrt_fusion), kind=kOutput, calls=%fused_computation.20 | convolution fusion | flops 540147712 | bytes 1838080 | tf_op jit(solution)/shard_map/tnh,hf->tnf/dot_general | solution.py:71
  54.8 3.5 %all-to-all-start.1 = ((bf16[16,32,256]{2,1,0:T(8,128)(2,1)}), bf16[16,32,256]{2,1,0:T(8,128)(2,1)S(1)}, u32[]{:S(2)}, u32[]{:S(2)}) async-start(bf16[16,32,256]{2,1,0:T(8,128)(2,1)} %fusion.16), calls=%async_computation.1 | async-start | bytes 524288 | tf_op jit(solution)/shard_map/all_to_all | solution.py:112
  58.4 7.3 %all-to-all-done.1 = bf16[16,32,256]{2,1,0:T(8,128)(2,1)S(1)} async-done(((bf16[16,32,256]{2,1,0:T(8,128)(2,1)}), bf16[16,32,256]{2,1,0:T(8,128)(2,1)S(1)}, u32[]{:S(2)}, u32[]{:S(2)}) %all-to-all-start.1) | async-done | bytes 262176 | tf_op jit(solution)/shard_map/all_to_all | solution.py:112
  65.6 5.6 %collective-permute-start.2 = (bf16[1,512,256]{2,1,0:T(8,128)(2,1)S(1)}, bf16[1,512,256]{2,1,0:T(8,128)(2,1)S(1)}, u32[]{:S(2)}, u32[]{:S(2)}) collective-permute-start(bf16[1,512,256]{2,1,0:T(8,128)(2,1)S(1)} %bitcast.108), channel_id=1, source_target_pairs={{0,1},{1,2},{2,3},{3,4},{4,5},{5,6},{6,7},{7,8},{8,9},{9,10},{10,1... | collective-permute-start | bytes 786440 | tf_op jit(solution)/shard_map/ppermute | solution.py:17
  71.3 1.9 %collective-permute-start.3 = (bf16[1,512,256]{2,1,0:T(8,128)(2,1)S(1)}, bf16[1,512,256]{2,1,0:T(8,128)(2,1)S(1)}, u32[]{:S(2)}, u32[]{:S(2)}) collective-permute-start(bf16[1,512,256]{2,1,0:T(8,128)(2,1)S(1)} %bitcast.109), channel_id=1, source_target_pairs={{1,0},{2,1},{3,2},{4,3},{5,4},{6,5},{7,6},{8,7},{9,8},{10,9},{11,1... | collective-permute-start | bytes 786440 | tf_op jit(solution)/shard_map/ppermute | solution.py:19
  73.2 0.2 convolution_convert_fusion
  73.5 2.0 %gather_fusion = bf16[32,128,256]{2,1,0:T(8,128)(2,1)} fusion(bf16[1,4,128,256]{3,2,1,0:T(8,128)(2,1)S(1)} %bitcast.103, s32[32]{0:T(128)S(1)} %or_bitcast_fusion.2), kind=kCustom, calls=%fused_computation.2 | custom fusion | bytes 4194560 | tf_op jit(solution)/shard_map/vmap(jit(_take))/gather | solution.py:35
  75.5 4.7 %collective-permute-done.3 = bf16[1,512,256]{2,1,0:T(8,128)(2,1)S(1)} collective-permute-done((bf16[1,512,256]{2,1,0:T(8,128)(2,1)S(1)}, bf16[1,512,256]{2,1,0:T(8,128)(2,1)S(1)}, u32[]{:S(2)}, u32[]{:S(2)}) %collective-permute-start.3) | collective-permute-done | bytes 262176 | tf_op jit(solution)/shard_map/ppermute | solution.py:19
  80.2 2.0 %gather_fusion.2 = bf16[32,128,256]{2,1,0:T(8,128)(2,1)} fusion(bf16[1,12,128,256]{3,2,1,0:T(8,128)(2,1)S(1)} %bitcast.105, s32[32]{0:T(128)S(1)} %or_bitcast_fusion), kind=kCustom, calls=%fused_computation.1.clone | custom fusion | bytes 4194560 | tf_op jit(solution)/shard_map/vmap(jit(_take))/gather | solution.py:35
  82.2 4.0 %fusion.11 = bf16[1,32,128,128]{3,2,1,0:T(8,128)(2,1)} fusion(bf16[32,128,256]{2,1,0:T(8,128)(2,1)} %gather_fusion.2, pred[32]{0:T(512)(128)(4,1)S(1)} %get-tuple-element.63, bf16[32,128,256]{2,1,0:T(8,128)(2,1)} %gather_fusion, pred[32]{0:T(512)(128)(4,1)S(1)} %get-tuple-element.69), kind=kOutput, calls=%fused_computation.18 | convolution fusion | flops 271581184 | bytes 5242944 | tf_op jit(solution)/shard_map/spif,spjf->spij/dot_general | solution.py:124
  86.2 0.7 copy.40
  (52 shorter events, 1.0 us)
Async XLA Ops:
  0.6 17.6 %copy-start = (bf16[1,32,128,128]{3,2,1,0:T(8,128)(2,1)S(1)}, bf16[1,32,128,128]{3,2,1,0:T(8,128)(2,1)}, u32[]{:S(2)}) copy-start(bf16[1,32,128,128]{3,2,1,0:T(8,128)(2,1)} %param.22) | copy-start | bytes 3145732
  0.6 10.1 %collective-permute-start = (bf16[1,512,256]{2,1,0:T(8,128)(2,1)}, bf16[1,512,256]{2,1,0:T(8,128)(2,1)S(1)}, u32[]{:S(2)}, u32[]{:S(2)}) collective-permute-start(bf16[1,512,256]{2,1,0:T(8,128)(2,1)} %param.18), channel_id=1, source_target_pairs={{0,1},{1,2},{2,3},{3,4},{4,5},{5,6},{6,7},{7,8},{8,9},{9,10},{10,1... | collective-permute-start | bytes 786440 | tf_op jit(solution)/shard_map/ppermute | solution.py:17
  6.1 9.1 %collective-permute-start.1 = (bf16[1,512,256]{2,1,0:T(8,128)(2,1)}, bf16[1,512,256]{2,1,0:T(8,128)(2,1)S(1)}, u32[]{:S(2)}, u32[]{:S(2)}) collective-permute-start(bf16[1,512,256]{2,1,0:T(8,128)(2,1)} %param.18), channel_id=1, source_target_pairs={{1,0},{2,1},{3,2},{4,3},{5,4},{6,5},{7,6},{8,7},{9,8},{10,9},{11,1... | collective-permute-start | bytes 786440 | tf_op jit(solution)/shard_map/ppermute | solution.py:19
  28.1 3.8 %copy-start.1 = (bf16[1,512,256]{2,1,0:T(8,128)(2,1)S(1)}, bf16[1,512,256]{2,1,0:T(8,128)(2,1)}, u32[]{:S(2)}) copy-start(bf16[1,512,256]{2,1,0:T(8,128)(2,1)} %param.18) | copy-start | bytes 786436
  28.1 4.0 %copy-start.4 = (f32[256]{0:T(256)S(1)}, f32[256]{0:T(256)}, u32[]{:S(2)}) copy-start(f32[256]{0:T(256)} %param.23) | copy-start | bytes 3076
  31.9 11.1 %copy-start.5 = (s32[1,32]{1,0:T(1,128)S(1)}, s32[1,32]{1,0:T(1,128)}, u32[]{:S(2)}) copy-start(s32[1,32]{1,0:T(1,128)} %param.31) | copy-start | bytes 388
  31.9 11.1 %copy-start.6 = (s32[1,32]{1,0:T(1,128)S(1)}, s32[1,32]{1,0:T(1,128)}, u32[]{:S(2)}) copy-start(s32[1,32]{1,0:T(1,128)} %param.30) | copy-start | bytes 388
  32.2 18.3 %copy-start.2 = (bf16[256,512]{1,0:T(8,128)(2,1)S(1)}, bf16[256,512]{1,0:T(8,128)(2,1)}, u32[]{:S(2)}) copy-start(bf16[256,512]{1,0:T(8,128)(2,1)} %param.24) | copy-start | bytes 786436
  36.2 14.1 %all-to-all-start = ((bf16[16,2,4096]{2,1,0:T(2,128)(2,1)}), bf16[16,2,4096]{2,1,0:T(2,128)(2,1)S(1)}, u32[]{:S(2)}, u32[]{:S(2)}) async-start(bf16[16,2,4096]{2,1,0:T(2,128)(2,1)} %reshape.205), calls=%async_computation | async-start | bytes 524288 | tf_op jit(solution)/shard_map/all_to_all | solution.py:108
  50.9 1.1 %copy-start.7 = (f32[256]{0:T(256)S(1)}, f32[256]{0:T(256)}, u32[]{:S(2)}) copy-start(f32[256]{0:T(256)} %param.26) | copy-start | bytes 3076
  52.0 21.3 %copy-start.3 = (bf16[256,256]{1,0:T(8,128)(2,1)S(1)}, bf16[256,256]{1,0:T(8,128)(2,1)}, u32[]{:S(2)}) copy-start(bf16[256,256]{1,0:T(8,128)(2,1)} %param.29) | copy-start | bytes 393220
  54.8 10.8 %all-to-all-start.1 = ((bf16[16,32,256]{2,1,0:T(8,128)(2,1)}), bf16[16,32,256]{2,1,0:T(8,128)(2,1)S(1)}, u32[]{:S(2)}, u32[]{:S(2)}) async-start(bf16[16,32,256]{2,1,0:T(8,128)(2,1)} %fusion.16), calls=%async_computation.1 | async-start | bytes 524288 | tf_op jit(solution)/shard_map/all_to_all | solution.py:112
  65.6 9.8 %collective-permute-start.2 = (bf16[1,512,256]{2,1,0:T(8,128)(2,1)S(1)}, bf16[1,512,256]{2,1,0:T(8,128)(2,1)S(1)}, u32[]{:S(2)}, u32[]{:S(2)}) collective-permute-start(bf16[1,512,256]{2,1,0:T(8,128)(2,1)S(1)} %bitcast.108), channel_id=1, source_target_pairs={{0,1},{1,2},{2,3},{3,4},{4,5},{5,6},{6,7},{7,8},{8,9},{9,10},{10,1... | collective-permute-start | bytes 786440 | tf_op jit(solution)/shard_map/ppermute | solution.py:17
  71.3 8.9 %collective-permute-start.3 = (bf16[1,512,256]{2,1,0:T(8,128)(2,1)S(1)}, bf16[1,512,256]{2,1,0:T(8,128)(2,1)S(1)}, u32[]{:S(2)}, u32[]{:S(2)}) collective-permute-start(bf16[1,512,256]{2,1,0:T(8,128)(2,1)S(1)} %bitcast.109), channel_id=1, source_target_pairs={{1,0},{2,1},{3,2},{4,3},{5,4},{6,5},{7,6},{8,7},{9,8},{10,9},{11,1... | collective-permute-start | bytes 786440 | tf_op jit(solution)/shard_map/ppermute | solution.py:19
where the time goes:
time: 87.6 us; the launch traced here: 86.9 us
  starting transfers between devices  25.2 us (29%)
  waiting for transfers between devices  23.7 us (27%)
  matrix products  15.4 us (18%)
  local copies, waits for them, and re-layouts  14.4 us (16%)
  other arithmetic  6.3 us (7%)
  between operations  1.6 us (2%)
    ppermute x2, starting transfers between devices, with_halo(): lax.ppermute(tail, axis, [(i, (i + 1) % count) for i in range(ends)])  11.1 us
    ppermute x2, waiting for transfers between devices, with_halo(): lax.ppermute(head, axis, [((i + 1) % count, i) for i in range(ends)])  9.16 us
    all_to_all x1, waiting for transfers between devices, body(): lax.all_to_all(vertex_out, 'snap', split_axis=0, concat_axis=1, tiled=True)  7.28 us
    all_to_all x1, waiting for transfers between devices, body(): lax.all_to_all(normed, 'snap', split_axis=1, concat_axis=0, tiled=True)  7.26 us
    all_to_all x1, starting transfers between devices, body(): lax.all_to_all(normed, 'snap', split_axis=1, concat_axis=0, tiled=True)  6.75 us
    gather x6, local copies, waits for them, and re-layouts, pick_blocks(): jnp.take(source_table, chosen, axis=0)  6.03 us
    dot_general x1, local copies, waits for them, and re-layouts, tile_terms(): jnp.einsum('sgij,sgjf->sgif', tile_part, picked, preferred_element_type=j...  5.47 us
    dot_general x1, matrix products, tile_terms(): jnp.einsum('sgij,sgjf->sgif', tile_part, picked, preferred_element_type=j...  4.37 us
  transfers between devices with their start and end apart: 6, of which 4 were waited for; matrix products, arithmetic and copies ran while one was open for 5% of the time, Pallas kernels for 0%

commit v1 on v0

--- a/solution.py
+++ b/solution.py
@@ -4,6 +4,34 @@
 from jax.sharding import PartitionSpec as P
 
 epsilon = 1e-06
+
+
+def _register_squares(frame, dim_at, panel):
+    high, seen_now = (frame.shape[:dim_at], frame.shape[dim_at + 1 :])
+    return jnp.moveaxis(frame.reshape(*high, panel, -1, *seen_now), dim_at, 0)
+
+
+def direct_area(vals, ndim_at):
+    vals = jnp.moveaxis(vals, 0, ndim_at)
+    n_now = vals.shape
+    return vals.reshape(
+        *n_now[:ndim_at], n_now[ndim_at] * n_now[ndim_at + 1], *n_now[ndim_at + 2 :]
+    )
+
+
+def edit_the_flows(array_here, group_axis, field, x_part):
+    current_block, big = (lax.axis_size(group_axis), lax.axis_index(group_axis))
+    q_next = _register_squares(array_here, field, current_block)
+    blocks_here = [q_next[big]]
+    for dev_i in range(1, current_block):
+        raw_out = q_next[big ^ dev_i]
+        blocks_here.append(
+            lax.ppermute(
+                raw_out, group_axis, [(to_i, to_i ^ dev_i) for to_i in range(current_block)]
+            )
+        )
+    q_next = jnp.stack(blocks_here, axis=0)[big ^ jnp.arange(current_block)]
+    return direct_area(q_next, x_part)
 
 
 def with_halo(cells, sides, width):
@@ -105,7 +133,7 @@
         jnp.float32
     )
     normed = root_norm(combined, norm_gain).astype(jnp.bfloat16)
-    by_vertex = lax.all_to_all(normed, "snap", split_axis=1, concat_axis=0, tiled=True)
+    by_vertex = edit_the_flows(normed, "snap", 1, 0)
     decays, drives = gate_drive(by_vertex, decay_rate, mix_weight)
     states = run_states(decays, drives, jnp.zeros(decays.shape[1:], jnp.float32))
     vertex_out = feed_forward(states, mlp_gain, up_weight, down_weight)

time: 87.6 us -> 135 us (1.54)
  starting transfers between devices: 25.2 us -> 76.7 us
  other arithmetic: 6.3 us -> 4.06 us
  waiting for transfers between devices: 23.7 us -> 22.3 us
    ppermute x0 -> x15, starting transfers between devices: none -> 55.9 us  [edit_the_flows(): lax.ppermute(raw_out, group_axis, [(to_i, to_i ^ dev_i) for to_i in range...]
    all_to_all x1 -> x0, waiting for transfers between devices: 7.26 us -> none  [body(): lax.all_to_all(normed, 'snap', split_axis=1, concat_axis=0, tiled=True)]
    all_to_all x1 -> x0, starting transfers between devices: 6.75 us -> none  [body(): lax.all_to_all(normed, 'snap', split_axis=1, concat_axis=0, tiled=True)]
    ppermute x0 -> x15, waiting for transfers between devices: none -> 5.81 us  [edit_the_flows(): lax.ppermute(raw_out, group_axis, [(to_i, to_i ^ dev_i) for to_i in range...]
    ppermute x2, starting transfers between devices: 11.1 us -> 13.5 us  [with_halo(): lax.ppermute(tail, axis, [(i, (i + 1) % count) for i in range(ends)])]
    unnamed x2 -> x1, other arithmetic: 2.21 us -> 0.01 us
    unnamed x21 -> x31, local copies, waits for them, and re-layouts: 2.34 us -> 0.8 us
  transfers between devices with their start and end apart: 6 -> 20, of which waited for: 4 -> 4; matrix products, arithmetic and copies ran while one was open for 5% -> 3% of each run, Pallas kernels for 0% -> 0%
where the time goes in v1:
time: 135 us; the launch traced here: 134 us
  starting transfers between devices  76.7 us (57%)
  waiting for transfers between devices  22.3 us (17%)
  matrix products  15.2 us (11%)
  local copies, waits for them, and re-layouts  13.1 us (10%)
  other arithmetic  4.06 us (3%)
  between operations  1.93 us (1%)
    ppermute x15, starting transfers between devices, edit_the_flows(): lax.ppermute(raw_out, group_axis, [(to_i, to_i ^ dev_i) for to_i in range...  55.9 us
    ppermute x2, starting transfers between devices, with_halo(): lax.ppermute(tail, axis, [(i, (i + 1) % count) for i in range(ends)])  13.5 us
    ppermute x2, waiting for transfers between devices, with_halo(): lax.ppermute(head, axis, [((i + 1) % count, i) for i in range(ends)])  9.19 us
    all_to_all x1, waiting for transfers between devices, body(): lax.all_to_all(vertex_out, 'snap', split_axis=0, concat_axis=1, tiled=True)  7.32 us
    gather x6, local copies, waits for them, and re-layouts, pick_blocks(): jnp.take(source_table, chosen, axis=0)  6.07 us
    ppermute x15, waiting for transfers between devices, edit_the_flows(): lax.ppermute(raw_out, group_axis, [(to_i, to_i ^ dev_i) for to_i in range...  5.81 us
    dot_general x1, local copies, waits for them, and re-layouts, tile_terms(): jnp.einsum('sgij,sgjf->sgif', tile_part, picked, preferred_element_type=j...  5.48 us
    dot_general x1, matrix products, tile_terms(): jnp.einsum('sgij,sgjf->sgif', tile_part, picked, preferred_element_type=j...  4.38 us
  transfers between devices with their start and end apart: 20, of which 4 were waited for; matrix products, arithmetic and copies ran while one was open for 3% of the time, Pallas kernels for 0%

profile of v1, /device:TPU:97, one launch (start us, length us, event | category | flops | bytes accessed | tf_op | source)
XLA Modules:
  0.0 133.8 jit_solution(10780688388732971505)
XLA Ops:
  0.6 5.5 %collective-permute-start = (bf16[1,512,256]{2,1,0:T(8,128)(2,1)}, bf16[1,512,256]{2,1,0:T(8,128)(2,1)S(1)}, u32[]{:S(2)}, u32[]{:S(2)}) collective-permute-start(bf16[1,512,256]{2,1,0:T(8,128)(2,1)} %param.18), channel_id=1, source_target_pairs={{0,1},{1,2},{2,3},{3,4},{4,5},{5,6},{6,7},{7,8},{8,9},{9,10},{10,1... | collective-permute-start | bytes 786440 | tf_op jit(solution)/shard_map/ppermute | solution.py:45
  6.1 1.9 %collective-permute-start.1 = (bf16[1,512,256]{2,1,0:T(8,128)(2,1)}, bf16[1,512,256]{2,1,0:T(8,128)(2,1)S(1)}, u32[]{:S(2)}, u32[]{:S(2)}) collective-permute-start(bf16[1,512,256]{2,1,0:T(8,128)(2,1)} %param.18), channel_id=1, source_target_pairs={{1,0},{2,1},{3,2},{4,3},{5,4},{6,5},{7,6},{8,7},{9,8},{10,9},{11,1... | collective-permute-start | bytes 786440 | tf_op jit(solution)/shard_map/ppermute | solution.py:47
  10.8 4.5 %collective-permute-done.1 = bf16[1,512,256]{2,1,0:T(8,128)(2,1)S(1)} collective-permute-done((bf16[1,512,256]{2,1,0:T(8,128)(2,1)}, bf16[1,512,256]{2,1,0:T(8,128)(2,1)S(1)}, u32[]{:S(2)}, u32[]{:S(2)}) %collective-permute-start.1) | collective-permute-done | bytes 262176 | tf_op jit(solution)/shard_map/ppermute | solution.py:47
  16.2 2.0 %gather_fusion.2 = bf16[32,128,256]{2,1,0:T(8,128)(2,1)} fusion(bf16[1,12,128,256]{3,2,1,0:T(8,128)(2,1)S(1)} %bitcast.163, s32[32]{0:T(128)S(1)} %or_bitcast_fusion.1), kind=kCustom, calls=%fused_computation.clone | custom fusion | bytes 4194560 | tf_op jit(solution)/shard_map/vmap(jit(_take))/gather | solution.py:63
  18.3 4.4 %fusion.4 = f32[32,256,128]{2,1,0:T(8,128)} fusion(bf16[32,128,256]{2,1,0:T(8,128)(2,1)} %gather_fusion.2, pred[32]{0:T(512)(128)(4,1)S(1)} %get-tuple-element.67, bf16[1,32,128,128]{3,2,1,0:T(8,128)(2,1)S(1)} %copy-done), kind=kOutput, calls=%fused_computation.12 | convolution fusion | flops 269484032 | bytes 7340064 | tf_op jit(solution)/shard_map/sgij,sgjf->sgif/dot_general | solution.py:70
  22.6 5.5 %copy.17 = f32[32,256,128]{1,0,2:T(8,128)} copy(f32[32,256,128]{2,1,0:T(8,128)} %fusion.4) | data formatting | bytes 8388608 | tf_op jit(solution)/shard_map/sgij,sgjf->sgif/dot_general | solution.py:70
  28.1 3.7 %fusion = f32[4,128,256]{2,0,1:T(4,128)S(1)} fusion(f32[32,256,128]{1,0,2:T(8,128)} %copy.17, s32[32]{0:T(128)S(1)} %subtract_bitcast_fusion, pred[32]{0:T(512)(128)(4,1)S(1)} %iota_compare_fusion.1), kind=kOutput, calls=%fused_computation.7 | convolution fusion | flops 50331904 | bytes 4718752 | tf_op jit(solution)/shard_map/sgb,sgif->sbif/dot_general | solution.py:73
  32.4 3.2 %collective-permute-start.2 = (bf16[1,32,256]{2,1,0:T(8,128)(2,1)S(1)}, bf16[1,32,256]{2,1,0:T(8,128)(2,1)S(1)}, u32[]{:S(2)}, u32[]{:S(2)}) collective-permute-start(bf16[1,32,256]{2,1,0:T(8,128)(2,1)S(1)} %get-tuple-element.83), channel_id=1, source_target_pairs={{0,32},{32,0},{64,96},{96,64},{128,160},{160,128},{192,224},{224,1... | collective-permute-start | bytes 49160 | tf_op jit(solution)/shard_map/ppermute | solution.py:29
  35.7 4.5 %collective-permute-start.3 = (bf16[1,32,256]{2,1,0:T(8,128)(2,1)S(1)}, bf16[1,32,256]{2,1,0:T(8,128)(2,1)S(1)}, u32[]{:S(2)}, u32[]{:S(2)}) collective-permute-start(bf16[1,32,256]{2,1,0:T(8,128)(2,1)S(1)} %get-tuple-element.82), channel_id=1, source_target_pairs={{0,64},{32,96},{64,0},{96,32},{128,192},{160,224},{192,128},{224,1... | collective-permute-start | bytes 49160 | tf_op jit(solution)/shard_map/ppermute | solution.py:29
  40.2 1.9 %collective-permute-start.4 = (bf16[1,32,256]{2,1,0:T(8,128)(2,1)S(1)}, bf16[1,32,256]{2,1,0:T(8,128)(2,1)S(1)}, u32[]{:S(2)}, u32[]{:S(2)}) collective-permute-start(bf16[1,32,256]{2,1,0:T(8,128)(2,1)S(1)} %get-tuple-element.81), channel_id=1, source_target_pairs={{0,96},{32,64},{64,32},{96,0},{128,224},{160,192},{192,160},{224,1... | collective-permute-start | bytes 49160 | tf_op jit(solution)/shard_map/ppermute | solution.py:29
  42.1 3.1 %collective-permute-start.5 = (bf16[1,32,256]{2,1,0:T(8,128)(2,1)S(1)}, bf16[1,32,256]{2,1,0:T(8,128)(2,1)S(1)}, u32[]{:S(2)}, u32[]{:S(2)}) collective-permute-start(bf16[1,32,256]{2,1,0:T(8,128)(2,1)S(1)} %get-tuple-element.80), channel_id=1, source_target_pairs={{0,128},{32,160},{64,192},{96,224},{128,0},{160,32},{192,64},{224,... | collective-permute-start | bytes 49160 | tf_op jit(solution)/shard_map/ppermute | solution.py:29
  45.3 1.9 %collective-permute-start.6 = (bf16[1,32,256]{2,1,0:T(8,128)(2,1)S(1)}, bf16[1,32,256]{2,1,0:T(8,128)(2,1)S(1)}, u32[]{:S(2)}, u32[]{:S(2)}) collective-permute-start(bf16[1,32,256]{2,1,0:T(8,128)(2,1)S(1)} %get-tuple-element.79), channel_id=1, source_target_pairs={{0,160},{32,128},{64,224},{96,192},{128,32},{160,0},{192,96},{224,... | collective-permute-start | bytes 49160 | tf_op jit(solution)/shard_map/ppermute | solution.py:29
  47.2 6.6 %collective-permute-start.7 = (bf16[1,32,256]{2,1,0:T(8,128)(2,1)S(1)}, bf16[1,32,256]{2,1,0:T(8,128)(2,1)S(1)}, u32[]{:S(2)}, u32[]{:S(2)}) collective-permute-start(bf16[1,32,256]{2,1,0:T(8,128)(2,1)S(1)} %get-tuple-element.78), channel_id=1, source_target_pairs={{0,192},{32,224},{64,128},{96,160},{128,64},{160,96},{192,0},{224,... | collective-permute-start | bytes 49160 | tf_op jit(solution)/shard_map/ppermute | solution.py:29
  53.9 1.9 %collective-permute-start.8 = (bf16[1,32,256]{2,1,0:T(8,128)(2,1)S(1)}, bf16[1,32,256]{2,1,0:T(8,128)(2,1)S(1)}, u32[]{:S(2)}, u32[]{:S(2)}) collective-permute-start(bf16[1,32,256]{2,1,0:T(8,128)(2,1)S(1)} %get-tuple-element.77), channel_id=1, source_target_pairs={{0,224},{32,192},{64,160},{96,128},{128,96},{160,64},{192,32},{224... | collective-permute-start | bytes 49160 | tf_op jit(solution)/shard_map/ppermute | solution.py:29
  55.8 4.6 %collective-permute-start.9 = (bf16[1,32,256]{2,1,0:T(8,128)(2,1)S(1)}, bf16[1,32,256]{2,1,0:T(8,128)(2,1)S(1)}, u32[]{:S(2)}, u32[]{:S(2)}) collective-permute-start(bf16[1,32,256]{2,1,0:T(8,128)(2,1)S(1)} %get-tuple-element.76), channel_id=1, source_target_pairs={{0,256},{32,288},{64,320},{96,352},{128,384},{160,416},{192,448},{... | collective-permute-start | bytes 49160 | tf_op jit(solution)/shard_map/ppermute | solution.py:29
  60.5 1.9 %collective-permute-start.10 = (bf16[1,32,256]{2,1,0:T(8,128)(2,1)S(1)}, bf16[1,32,256]{2,1,0:T(8,128)(2,1)S(1)}, u32[]{:S(2)}, u32[]{:S(2)}) collective-permute-start(bf16[1,32,256]{2,1,0:T(8,128)(2,1)S(1)} %get-tuple-element.75), channel_id=1, source_target_pairs={{0,288},{32,256},{64,352},{96,320},{128,416},{160,384},{192,480},{... | collective-permute-start | bytes 49160 | tf_op jit(solution)/shard_map/ppermute | solution.py:29
  62.4 8.1 %collective-permute-start.11 = (bf16[1,32,256]{2,1,0:T(8,128)(2,1)S(1)}, bf16[1,32,256]{2,1,0:T(8,128)(2,1)S(1)}, u32[]{:S(2)}, u32[]{:S(2)}) collective-permute-start(bf16[1,32,256]{2,1,0:T(8,128)(2,1)S(1)} %get-tuple-element.74), channel_id=1, source_target_pairs={{0,320},{32,352},{64,256},{96,288},{128,448},{160,480},{192,384},{... | collective-permute-start | bytes 49160 | tf_op jit(solution)/shard_map/ppermute | solution.py:29
  70.6 1.9 %collective-permute-start.12 = (bf16[1,32,256]{2,1,0:T(8,128)(2,1)S(1)}, bf16[1,32,256]{2,1,0:T(8,128)(2,1)S(1)}, u32[]{:S(2)}, u32[]{:S(2)}) collective-permute-start(bf16[1,32,256]{2,1,0:T(8,128)(2,1)S(1)} %get-tuple-element.73), channel_id=1, source_target_pairs={{0,352},{32,320},{64,288},{96,256},{128,480},{160,448},{192,416},{... | collective-permute-start | bytes 49160 | tf_op jit(solution)/shard_map/ppermute | solution.py:29
  72.6 4.3 %collective-permute-start.13 = (bf16[1,32,256]{2,1,0:T(8,128)(2,1)S(1)}, bf16[1,32,256]{2,1,0:T(8,128)(2,1)S(1)}, u32[]{:S(2)}, u32[]{:S(2)}) collective-permute-start(bf16[1,32,256]{2,1,0:T(8,128)(2,1)S(1)} %get-tuple-element.72), channel_id=1, source_target_pairs={{0,384},{32,416},{64,448},{96,480},{128,256},{160,288},{192,320},{... | collective-permute-start | bytes 49160 | tf_op jit(solution)/shard_map/ppermute | solution.py:29
  76.9 1.9 %collective-permute-start.14 = (bf16[1,32,256]{2,1,0:T(8,128)(2,1)S(1)}, bf16[1,32,256]{2,1,0:T(8,128)(2,1)S(1)}, u32[]{:S(2)}, u32[]{:S(2)}) collective-permute-start(bf16[1,32,256]{2,1,0:T(8,128)(2,1)S(1)} %get-tuple-element.71), channel_id=1, source_target_pairs={{0,416},{32,384},{64,480},{96,448},{128,288},{160,256},{192,352},{... | collective-permute-start | bytes 49160 | tf_op jit(solution)/shard_map/ppermute | solution.py:29
  78.9 7.9 %collective-permute-start.15 = (bf16[1,32,256]{2,1,0:T(8,128)(2,1)S(1)}, bf16[1,32,256]{2,1,0:T(8,128)(2,1)S(1)}, u32[]{:S(2)}, u32[]{:S(2)}) collective-permute-start(bf16[1,32,256]{2,1,0:T(8,128)(2,1)S(1)} %get-tuple-element.70), channel_id=1, source_target_pairs={{0,448},{32,480},{64,384},{96,416},{128,320},{160,352},{192,256},{... | collective-permute-start | bytes 49160 | tf_op jit(solution)/shard_map/ppermute | solution.py:29
  86.8 1.9 %collective-permute-start.16 = (bf16[1,32,256]{2,1,0:T(8,128)(2,1)S(1)}, bf16[1,32,256]{2,1,0:T(8,128)(2,1)S(1)}, u32[]{:S(2)}, u32[]{:S(2)}) collective-permute-start(bf16[1,32,256]{2,1,0:T(8,128)(2,1)S(1)} %get-tuple-element.69), channel_id=1, source_target_pairs={{0,480},{32,448},{64,416},{96,384},{128,352},{160,320},{192,288},{... | collective-permute-start | bytes 49160 | tf_op jit(solution)/shard_map/ppermute | solution.py:29
  88.8 5.8 %collective-permute-done.16 = bf16[1,32,256]{2,1,0:T(8,128)(2,1)S(1)} collective-permute-done((bf16[1,32,256]{2,1,0:T(8,128)(2,1)S(1)}, bf16[1,32,256]{2,1,0:T(8,128)(2,1)S(1)}, u32[]{:S(2)}, u32[]{:S(2)}) %collective-permute-start.16) | collective-permute-done | bytes 16416 | tf_op jit(solution)/shard_map/ppermute | solution.py:29
  96.5 2.7 %fusion.19 = bf16[16,32,256]{2,1,0:T(8,128)(2,1)} fusion(f32[16,32,256]{2,1,0:T(8,128)S(1)} %get-tuple-element.30, bf16[1024,256]{1,0:T(8,128)(2,1)S(1)} %copy-done.6, bf16[256,1024]{1,0:T(8,128)(2,1)} %param.27, f32[256]{0:T(256)S(1)} %copy-done.7, f32[16,32]{1,0:T(8,128)S(1)} %add_rsqrt_fusion), kind=kOutput, calls=%fused_computation.23 | convolution fusion | flops 540147712 | bytes 1838080 | tf_op jit(solution)/shard_map/tnh,hf->tnf/dot_general | solution.py:99
  99.2 3.5 %all-to-all-start = ((bf16[16,32,256]{2,1,0:T(8,128)(2,1)}), bf16[16,32,256]{2,1,0:T(8,128)(2,1)S(1)}, u32[]{:S(2)}, u32[]{:S(2)}) async-start(bf16[16,32,256]{2,1,0:T(8,128)(2,1)} %fusion.19), calls=%async_computation | async-start | bytes 524288 | tf_op jit(solution)/shard_map/all_to_all | solution.py:140
  102.8 7.3 %all-to-all-done = bf16[16,32,256]{2,1,0:T(8,128)(2,1)S(1)} async-done(((bf16[16,32,256]{2,1,0:T(8,128)(2,1)}), bf16[16,32,256]{2,1,0:T(8,128)(2,1)S(1)}, u32[]{:S(2)}, u32[]{:S(2)}) %all-to-all-start) | async-done | bytes 262176 | tf_op jit(solution)/shard_map/all_to_all | solution.py:140
  110.1 8.0 %collective-permute-start.17 = (bf16[1,512,256]{2,1,0:T(8,128)(2,1)S(1)}, bf16[1,512,256]{2,1,0:T(8,128)(2,1)S(1)}, u32[]{:S(2)}, u32[]{:S(2)}) collective-permute-start(bf16[1,512,256]{2,1,0:T(8,128)(2,1)S(1)} %bitcast.167), channel_id=1, source_target_pairs={{0,1},{1,2},{2,3},{3,4},{4,5},{5,6},{6,7},{7,8},{8,9},{9,10},{10,1... | collective-permute-start | bytes 786440 | tf_op jit(solution)/shard_map/ppermute | solution.py:45
  118.1 1.9 %collective-permute-start.18 = (bf16[1,512,256]{2,1,0:T(8,128)(2,1)S(1)}, bf16[1,512,256]{2,1,0:T(8,128)(2,1)S(1)}, u32[]{:S(2)}, u32[]{:S(2)}) collective-permute-start(bf16[1,512,256]{2,1,0:T(8,128)(2,1)S(1)} %bitcast.168), channel_id=1, source_target_pairs={{1,0},{2,1},{3,2},{4,3},{5,4},{6,5},{7,6},{8,7},{9,8},{10,9},{11,1... | collective-permute-start | bytes 786440 | tf_op jit(solution)/shard_map/ppermute | solution.py:47
  120.3 2.0 %gather_fusion.1 = bf16[32,128,256]{2,1,0:T(8,128)(2,1)} fusion(bf16[1,4,128,256]{3,2,1,0:T(8,128)(2,1)S(1)} %bitcast.162, s32[32]{0:T(128)S(1)} %or_bitcast_fusion.2), kind=kCustom, calls=%fused_computation.3 | custom fusion | bytes 4194560 | tf_op jit(solution)/shard_map/vmap(jit(_take))/gather | solution.py:63
  122.3 4.7 %collective-permute-done.18 = bf16[1,512,256]{2,1,0:T(8,128)(2,1)S(1)} collective-permute-done((bf16[1,512,256]{2,1,0:T(8,128)(2,1)S(1)}, bf16[1,512,256]{2,1,0:T(8,128)(2,1)S(1)}, u32[]{:S(2)}, u32[]{:S(2)}) %collective-permute-start.18) | collective-permute-done | bytes 262176 | tf_op jit(solution)/shard_map/ppermute | solution.py:47
  127.1 2.0 %gather_fusion.3 = bf16[32,128,256]{2,1,0:T(8,128)(2,1)} fusion(bf16[1,12,128,256]{3,2,1,0:T(8,128)(2,1)S(1)} %bitcast.164, s32[32]{0:T(128)S(1)} %or_bitcast_fusion), kind=kCustom, calls=%fused_computation.1.clone | custom fusion | bytes 4194560 | tf_op jit(solution)/shard_map/vmap(jit(_take))/gather | solution.py:63
  129.1 4.0 %fusion.14 = bf16[1,32,128,128]{3,2,1,0:T(8,128)(2,1)} fusion(bf16[32,128,256]{2,1,0:T(8,128)(2,1)} %gather_fusion.3, pred[32]{0:T(512)(128)(4,1)S(1)} %get-tuple-element.63, bf16[32,128,256]{2,1,0:T(8,128)(2,1)} %gather_fusion.1, pred[32]{0:T(512)(128)(4,1)S(1)} %get-tuple-element.85), kind=kOutput, calls=%fused_computation.21 | convolution fusion | flops 271581184 | bytes 5242944 | tf_op jit(solution)/shard_map/spif,spjf->spij/dot_general | solution.py:152
  (93 shorter events, 6.8 us)
Async XLA Ops:
  0.6 17.6 %copy-start = (bf16[1,32,128,128]{3,2,1,0:T(8,128)(2,1)S(1)}, bf16[1,32,128,128]{3,2,1,0:T(8,128)(2,1)}, u32[]{:S(2)}) copy-start(bf16[1,32,128,128]{3,2,1,0:T(8,128)(2,1)} %param.22) | copy-start | bytes 3145732
  0.6 10.1 %collective-permute-start = (bf16[1,512,256]{2,1,0:T(8,128)(2,1)}, bf16[1,512,256]{2,1,0:T(8,128)(2,1)S(1)}, u32[]{:S(2)}, u32[]{:S(2)}) collective-permute-start(bf16[1,512,256]{2,1,0:T(8,128)(2,1)} %param.18), channel_id=1, source_target_pairs={{0,1},{1,2},{2,3},{3,4},{4,5},{5,6},{6,7},{7,8},{8,9},{9,10},{10,1... | collective-permute-start | bytes 786440 | tf_op jit(solution)/shard_map/ppermute | solution.py:45
  6.1 9.1 %collective-permute-start.1 = (bf16[1,512,256]{2,1,0:T(8,128)(2,1)}, bf16[1,512,256]{2,1,0:T(8,128)(2,1)S(1)}, u32[]{:S(2)}, u32[]{:S(2)}) collective-permute-start(bf16[1,512,256]{2,1,0:T(8,128)(2,1)} %param.18), channel_id=1, source_target_pairs={{1,0},{2,1},{3,2},{4,3},{5,4},{6,5},{7,6},{8,7},{9,8},{10,9},{11,1... | collective-permute-start | bytes 786440 | tf_op jit(solution)/shard_map/ppermute | solution.py:47
  28.1 3.8 %copy-start.1 = (bf16[1,512,256]{2,1,0:T(8,128)(2,1)S(1)}, bf16[1,512,256]{2,1,0:T(8,128)(2,1)}, u32[]{:S(2)}) copy-start(bf16[1,512,256]{2,1,0:T(8,128)(2,1)} %param.18) | copy-start | bytes 786436
  28.1 4.0 %copy-start.5 = (f32[256]{0:T(256)S(1)}, f32[256]{0:T(256)}, u32[]{:S(2)}) copy-start(f32[256]{0:T(256)} %param.23) | copy-start | bytes 3076
  31.8 3.8 %copy-start.4 = (f32[16,256]{1,0:T(8,128)S(1)}, f32[16,256]{1,0:T(8,128)}, u32[]{:S(2)}) copy-start(f32[16,256]{1,0:T(8,128)} %param.25) | copy-start | bytes 49156
  31.8 63.3 %copy-start.2 = (bf16[256,512]{1,0:T(8,128)(2,1)S(1)}, bf16[256,512]{1,0:T(8,128)(2,1)}, u32[]{:S(2)}) copy-start(bf16[256,512]{1,0:T(8,128)(2,1)} %param.24) | copy-start | bytes 786436
  32.4 14.8 %collective-permute-start.2 = (bf16[1,32,256]{2,1,0:T(8,128)(2,1)S(1)}, bf16[1,32,256]{2,1,0:T(8,128)(2,1)S(1)}, u32[]{:S(2)}, u32[]{:S(2)}) collective-permute-start(bf16[1,32,256]{2,1,0:T(8,128)(2,1)S(1)} %get-tuple-element.83), channel_id=1, source_target_pairs={{0,32},{32,0},{64,96},{96,64},{128,160},{160,128},{192,224},{224,1... | collective-permute-start | bytes 49160 | tf_op jit(solution)/shard_map/ppermute | solution.py:29
  35.7 18.2 %collective-permute-start.3 = (bf16[1,32,256]{2,1,0:T(8,128)(2,1)S(1)}, bf16[1,32,256]{2,1,0:T(8,128)(2,1)S(1)}, u32[]{:S(2)}, u32[]{:S(2)}) collective-permute-start(bf16[1,32,256]{2,1,0:T(8,128)(2,1)S(1)} %get-tuple-element.82), channel_id=1, source_target_pairs={{0,64},{32,96},{64,0},{96,32},{128,192},{160,224},{192,128},{224,1... | collective-permute-start | bytes 49160 | tf_op jit(solution)/shard_map/ppermute | solution.py:29
  40.2 15.6 %collective-permute-start.4 = (bf16[1,32,256]{2,1,0:T(8,128)(2,1)S(1)}, bf16[1,32,256]{2,1,0:T(8,128)(2,1)S(1)}, u32[]{:S(2)}, u32[]{:S(2)}) collective-permute-start(bf16[1,32,256]{2,1,0:T(8,128)(2,1)S(1)} %get-tuple-element.81), channel_id=1, source_target_pairs={{0,96},{32,64},{64,32},{96,0},{128,224},{160,192},{192,160},{224,1... | collective-permute-start | bytes 49160 | tf_op jit(solution)/shard_map/ppermute | solution.py:29
  42.1 18.3 %collective-permute-start.5 = (bf16[1,32,256]{2,1,0:T(8,128)(2,1)S(1)}, bf16[1,32,256]{2,1,0:T(8,128)(2,1)S(1)}, u32[]{:S(2)}, u32[]{:S(2)}) collective-permute-start(bf16[1,32,256]{2,1,0:T(8,128)(2,1)S(1)} %get-tuple-element.80), channel_id=1, source_target_pairs={{0,128},{32,160},{64,192},{96,224},{128,0},{160,32},{192,64},{224,... | collective-permute-start | bytes 49160 | tf_op jit(solution)/shard_map/ppermute | solution.py:29
  45.3 17.2 %collective-permute-start.6 = (bf16[1,32,256]{2,1,0:T(8,128)(2,1)S(1)}, bf16[1,32,256]{2,1,0:T(8,128)(2,1)S(1)}, u32[]{:S(2)}, u32[]{:S(2)}) collective-permute-start(bf16[1,32,256]{2,1,0:T(8,128)(2,1)S(1)} %get-tuple-element.79), channel_id=1, source_target_pairs={{0,160},{32,128},{64,224},{96,192},{128,32},{160,0},{192,96},{224,... | collective-permute-start | bytes 49160 | tf_op jit(solution)/shard_map/ppermute | solution.py:29
  47.2 23.4 %collective-permute-start.7 = (bf16[1,32,256]{2,1,0:T(8,128)(2,1)S(1)}, bf16[1,32,256]{2,1,0:T(8,128)(2,1)S(1)}, u32[]{:S(2)}, u32[]{:S(2)}) collective-permute-start(bf16[1,32,256]{2,1,0:T(8,128)(2,1)S(1)} %get-tuple-element.78), channel_id=1, source_target_pairs={{0,192},{32,224},{64,128},{96,160},{128,64},{160,96},{192,0},{224,... | collective-permute-start | bytes 49160 | tf_op jit(solution)/shard_map/ppermute | solution.py:29
  53.9 18.7 %collective-permute-start.8 = (bf16[1,32,256]{2,1,0:T(8,128)(2,1)S(1)}, bf16[1,32,256]{2,1,0:T(8,128)(2,1)S(1)}, u32[]{:S(2)}, u32[]{:S(2)}) collective-permute-start(bf16[1,32,256]{2,1,0:T(8,128)(2,1)S(1)} %get-tuple-element.77), channel_id=1, source_target_pairs={{0,224},{32,192},{64,160},{96,128},{128,96},{160,64},{192,32},{224... | collective-permute-start | bytes 49160 | tf_op jit(solution)/shard_map/ppermute | solution.py:29
  55.8 21.1 %collective-permute-start.9 = (bf16[1,32,256]{2,1,0:T(8,128)(2,1)S(1)}, bf16[1,32,256]{2,1,0:T(8,128)(2,1)S(1)}, u32[]{:S(2)}, u32[]{:S(2)}) collective-permute-start(bf16[1,32,256]{2,1,0:T(8,128)(2,1)S(1)} %get-tuple-element.76), channel_id=1, source_target_pairs={{0,256},{32,288},{64,320},{96,352},{128,384},{160,416},{192,448},{... | collective-permute-start | bytes 49160 | tf_op jit(solution)/shard_map/ppermute | solution.py:29
  60.5 18.4 %collective-permute-start.10 = (bf16[1,32,256]{2,1,0:T(8,128)(2,1)S(1)}, bf16[1,32,256]{2,1,0:T(8,128)(2,1)S(1)}, u32[]{:S(2)}, u32[]{:S(2)}) collective-permute-start(bf16[1,32,256]{2,1,0:T(8,128)(2,1)S(1)} %get-tuple-element.75), channel_id=1, source_target_pairs={{0,288},{32,256},{64,352},{96,320},{128,416},{160,384},{192,480},{... | collective-permute-start | bytes 49160 | tf_op jit(solution)/shard_map/ppermute | solution.py:29
  62.4 24.3 %collective-permute-start.11 = (bf16[1,32,256]{2,1,0:T(8,128)(2,1)S(1)}, bf16[1,32,256]{2,1,0:T(8,128)(2,1)S(1)}, u32[]{:S(2)}, u32[]{:S(2)}) collective-permute-start(bf16[1,32,256]{2,1,0:T(8,128)(2,1)S(1)} %get-tuple-element.74), channel_id=1, source_target_pairs={{0,320},{32,352},{64,256},{96,288},{128,448},{160,480},{192,384},{... | collective-permute-start | bytes 49160 | tf_op jit(solution)/shard_map/ppermute | solution.py:29
  70.6 18.1 %collective-permute-start.12 = (bf16[1,32,256]{2,1,0:T(8,128)(2,1)S(1)}, bf16[1,32,256]{2,1,0:T(8,128)(2,1)S(1)}, u32[]{:S(2)}, u32[]{:S(2)}) collective-permute-start(bf16[1,32,256]{2,1,0:T(8,128)(2,1)S(1)} %get-tuple-element.73), channel_id=1, source_target_pairs={{0,352},{32,320},{64,288},{96,256},{128,480},{160,448},{192,416},{... | collective-permute-start | bytes 49160 | tf_op jit(solution)/shard_map/ppermute | solution.py:29
  72.6 16.2 %collective-permute-start.13 = (bf16[1,32,256]{2,1,0:T(8,128)(2,1)S(1)}, bf16[1,32,256]{2,1,0:T(8,128)(2,1)S(1)}, u32[]{:S(2)}, u32[]{:S(2)}) collective-permute-start(bf16[1,32,256]{2,1,0:T(8,128)(2,1)S(1)} %get-tuple-element.72), channel_id=1, source_target_pairs={{0,384},{32,416},{64,448},{96,480},{128,256},{160,288},{192,320},{... | collective-permute-start | bytes 49160 | tf_op jit(solution)/shard_map/ppermute | solution.py:29
  76.9 11.8 %collective-permute-start.14 = (bf16[1,32,256]{2,1,0:T(8,128)(2,1)S(1)}, bf16[1,32,256]{2,1,0:T(8,128)(2,1)S(1)}, u32[]{:S(2)}, u32[]{:S(2)}) collective-permute-start(bf16[1,32,256]{2,1,0:T(8,128)(2,1)S(1)} %get-tuple-element.71), channel_id=1, source_target_pairs={{0,416},{32,384},{64,480},{96,448},{128,288},{160,256},{192,352},{... | collective-permute-start | bytes 49160 | tf_op jit(solution)/shard_map/ppermute | solution.py:29
  78.9 9.9 %collective-permute-start.15 = (bf16[1,32,256]{2,1,0:T(8,128)(2,1)S(1)}, bf16[1,32,256]{2,1,0:T(8,128)(2,1)S(1)}, u32[]{:S(2)}, u32[]{:S(2)}) collective-permute-start(bf16[1,32,256]{2,1,0:T(8,128)(2,1)S(1)} %get-tuple-element.70), channel_id=1, source_target_pairs={{0,448},{32,480},{64,384},{96,416},{128,320},{160,352},{192,256},{... | collective-permute-start | bytes 49160 | tf_op jit(solution)/shard_map/ppermute | solution.py:29
  86.8 7.8 %collective-permute-start.16 = (bf16[1,32,256]{2,1,0:T(8,128)(2,1)S(1)}, bf16[1,32,256]{2,1,0:T(8,128)(2,1)S(1)}, u32[]{:S(2)}, u32[]{:S(2)}) collective-permute-start(bf16[1,32,256]{2,1,0:T(8,128)(2,1)S(1)} %get-tuple-element.69), channel_id=1, source_target_pairs={{0,480},{32,448},{64,416},{96,384},{128,352},{160,320},{192,288},{... | collective-permute-start | bytes 49160 | tf_op jit(solution)/shard_map/ppermute | solution.py:29
  95.4 1.1 copy-start.6
  95.4 1.1 copy-start.7
  96.5 23.5 %copy-start.3 = (bf16[256,256]{1,0:T(8,128)(2,1)S(1)}, bf16[256,256]{1,0:T(8,128)(2,1)}, u32[]{:S(2)}) copy-start(bf16[256,256]{1,0:T(8,128)(2,1)} %param.29) | copy-start | bytes 393220
  99.2 10.9 %all-to-all-start = ((bf16[16,32,256]{2,1,0:T(8,128)(2,1)}), bf16[16,32,256]{2,1,0:T(8,128)(2,1)S(1)}, u32[]{:S(2)}, u32[]{:S(2)}) async-start(bf16[16,32,256]{2,1,0:T(8,128)(2,1)} %fusion.19), calls=%async_computation | async-start | bytes 524288 | tf_op jit(solution)/shard_map/all_to_all | solution.py:140
  110.1 12.2 %collective-permute-start.17 = (bf16[1,512,256]{2,1,0:T(8,128)(2,1)S(1)}, bf16[1,512,256]{2,1,0:T(8,128)(2,1)S(1)}, u32[]{:S(2)}, u32[]{:S(2)}) collective-permute-start(bf16[1,512,256]{2,1,0:T(8,128)(2,1)S(1)} %bitcast.167), channel_id=1, source_target_pairs={{0,1},{1,2},{2,3},{3,4},{4,5},{5,6},{6,7},{7,8},{8,9},{9,10},{10,1... | collective-permute-start | bytes 786440 | tf_op jit(solution)/shard_map/ppermute | solution.py:45
  118.1 8.9 %collective-permute-start.18 = (bf16[1,512,256]{2,1,0:T(8,128)(2,1)S(1)}, bf16[1,512,256]{2,1,0:T(8,128)(2,1)S(1)}, u32[]{:S(2)}, u32[]{:S(2)}) collective-permute-start(bf16[1,512,256]{2,1,0:T(8,128)(2,1)S(1)} %bitcast.168), channel_id=1, source_target_pairs={{1,0},{2,1},{3,2},{4,3},{5,4},{6,5},{7,6},{8,7},{9,8},{10,9},{11,1... | collective-permute-start | bytes 786440 | tf_op jit(solution)/shard_map/ppermute | solution.py:47
